TPU v7x, 32 devices: a whole 2x2x4 slice. The times are simulated.
32 devices in a mesh: groups: 1, kcol: 16 (over z, y, x), qrow: 2 (over core).
Axes of the slice: x: 2, y: 2, z: 4, core: 2. Of those that a mesh axis runs over, the one named last changes fastest.
Arguments:
- queries: bfloat16 [128, 1024], P(('groups', 'kcol', 'qrow')), may hold values from -120 to 120
- key_value: bfloat16 [24576, 256], P(('groups', 'kcol')), may hold values from -6 to 6
- block_lists: int32 [1, 64], P('groups'), may hold values from 0 to 191, as said below
Outputs:
- attended: bfloat16 [128, 1024], P(('groups', 'kcol', 'qrow'))
Inputs may be any that keep to these rules, and one draw needn't show every extreme that they name: `block_lists`: row i names 64 distinct key blocks, none after block 191 + i (the block that holds query block i); it always names that block, the 11 blocks just before it, and block 0.
All inputs are finite; a program needn't handle non-finite values.
Results may differ from a plain program's by a relative error of at most 0.0065.
Values may be sent and summed in bfloat16 or wider, within the bound.
A program may use at most 128 MiB of HBM per device.

v0:
```python
import math

import jax
import jax.numpy as jnp
from jax import lax
from jax.sharding import PartitionSpec as P

BLK = 128


masked_score = -1e30


def combined_all(part, axis, combine):
    gathered = jax.tree.map(lambda a: lax.all_gather(a, axis), part)

    def take(source):
        return jax.tree.map(lambda a: lax.dynamic_index_in_dim(a, source, 0, False), gathered)

    return lax.fori_loop(
        1, lax.axis_size(axis), lambda source, state: combine(state, take(source)), take(0)
    )


def partial_softmax(query_tile, key_rows, value_rows, visible):
    score_scale = 1.0 / math.sqrt(key_rows.shape[1])
    scores = (
        jnp.einsum("thd,kd->htk", query_tile, key_rows, preferred_element_type=jnp.float32)
        * score_scale
    )
    scores = jnp.where(visible[None], scores, masked_score)
    row_max = jnp.max(scores, axis=-1)
    weights = jnp.where(visible[None], jnp.exp(scores - row_max[..., None]), 0.0)
    row_total = jnp.sum(weights, axis=-1)
    numerator = jnp.einsum(
        "htk,kd->thd", weights.astype(jnp.bfloat16), value_rows, preferred_element_type=jnp.float32
    )
    return (jnp.transpose(row_max), jnp.transpose(row_total), numerator)


def combine_partials(left_part, right_part):
    max_left, total_left, numer_left = left_part
    max_right, total_right, numer_right = right_part
    row_max = jnp.maximum(max_left, max_right)
    scale_left = jnp.exp(max_left - row_max)
    scale_right = jnp.exp(max_right - row_max)
    return (
        row_max,
        total_left * scale_left + total_right * scale_right,
        numer_left * scale_left[..., None] + numer_right * scale_right[..., None],
    )


def per_device(queries, key_value, block_lists):
    column_count = lax.axis_size("kcol")
    column = lax.axis_index("kcol")
    row_count = lax.axis_size("qrow")
    row_index = lax.axis_index("qrow")
    tok_dev = queries.shape[0]
    feature_count = queries.shape[1]
    head_dim = key_value.shape[1] // 2
    head_count = feature_count // head_dim
    stored = key_value.shape[0] // BLK
    all_blocks = stored * column_count
    gathered = lax.all_gather(queries, "kcol", axis=0, tiled=True)
    gathered_rows = gathered.shape[0]
    tile_rows = BLK // row_count
    query_blocks = gathered_rows // tile_rows
    offset = (all_blocks - query_blocks) * BLK
    gather_pos = jnp.arange(gathered_rows, dtype=jnp.int32)
    token_index = (gather_pos // tok_dev * row_count + row_index) * tok_dev + gather_pos % tok_dev
    query_pos = (offset + token_index).reshape(query_blocks, tile_rows)
    query_tiles = gathered.reshape(query_blocks, tile_rows, head_count, head_dim)
    block_ids = column * stored + jnp.arange(stored, dtype=jnp.int32)
    key_pos = column * stored * BLK + jnp.arange(stored * BLK, dtype=jnp.int32)
    key_rows = key_value[:, :head_dim]
    value_rows = key_value[:, head_dim:]

    def one_block(inputs):
        query_tile, positions, listed = inputs
        listed_here = jnp.any(listed[:, None] == block_ids[None, :], axis=0)
        usable = jnp.repeat(listed_here, BLK, total_repeat_length=stored * BLK)
        visible = usable[None, :] & (key_pos[None, :] <= positions[:, None])
        return partial_softmax(query_tile, key_rows, value_rows, visible)

    row_max, row_total, numerator = lax.map(one_block, (query_tiles, query_pos, block_lists))
    row_max = row_max.reshape(gathered_rows, head_count)
    row_total = row_total.reshape(gathered_rows, head_count)
    numerator = numerator.reshape(gathered_rows, head_count, head_dim)
    merged = combined_all((row_max, row_total, numerator), "kcol", combine_partials)
    first_row = column * tok_dev
    summed_total = lax.dynamic_slice_in_dim(merged[1], first_row, tok_dev, 0)
    summed_numer = lax.dynamic_slice_in_dim(merged[2], first_row, tok_dev, 0)
    attended = summed_numer / summed_total[..., None]
    return attended.reshape(tok_dev, feature_count).astype(jnp.bfloat16)


def solution(mesh):
    placed = (P(("groups", "kcol", "qrow"), None), P(("groups", "kcol"), None), P("groups", None))
    return jax.shard_map(
        per_device,
        mesh=mesh,
        in_specs=placed,
        out_specs=P(("groups", "kcol", "qrow"), None),
        check_vma=False,
    )
```

profile of v0, /device:TPU:0, one launch (start us, length us, event | category | flops | bytes accessed | tf_op | source)
XLA Modules:
  0.0 169.0 jit_solution(10916630586948243898)
XLA Ops:
  6.6 0.8 compare_reduce_fusion.5
  7.4 0.7 fusion.37
  8.1 43.3 %all-gather.3 = bf16[16,4,1024]{2,1,0:T(4,128)(2,1)S(1)} all-gather(bf16[1,4,1024]{2,1,0:T(4,128)(2,1)} %bitcast.104), channel_id=1, replica_groups=mesh['groups'=1,'kcol'=16,'qrow'=2] {'kcol'}, dimensions={0}, use_global_device_ids=true | all-gather | bytes 139264 | tf_op jit(solution)/shard_map/all_gather | solution.py:65
  51.5 4.5 %select_reduce_fusion = (pred[1536]{0:T(1024)(128)(4,1)S(1)}, pred[1536]{0:T(1024)(128)(4,1)S(1)}, pred[1536]{0:T(1024)(128)(4,1)S(1)}, pred[1536]{0:T(1024)(128...) fusion(pred[]{:T(512)} %bitcast.11, pred[]{:T(512)} %bitcast.12, pred[]{:T(512)} %bitcast.13, ...), kind=kLoop, calls=%fused_computation.28 | loop fusion | flops 29184 | bytes 21511 | tf_op jit(solution)/shard_map/while/body/eval_jaxpr/jit(_take)/gather | solution.py:82
  56.0 3.2 %fusion.29 = pred[1536]{0:T(1024)(128)(4,1)S(1)} fusion(pred[1536]{0:T(1024)(128)(4,1)S(1)} %get-tuple-element.267, pred[1536]{0:T(1024)(128)(4,1)S(1)} %get-tuple-element.266, pred[1536]{0:T(1024)(128)(4,1)S(1)} %get-tuple-element.265, pred[1536]{0:T(1024)(128)(4,1)S(1)} %get-tuple-element.263, pred[1536]{0:T(1024)(128)(4,1)S(1)} %get-tuple-element.264, ...), kind=kLoop, calls=%fused_computation.47 | loop fusion | flops 21504 | bytes 10757 | tf_op jit(solution)/shard_map/while/body/eval_jaxpr/jit(_take)/select_n | solution.py:82
  59.4 1.7 %fusion.38 = (f32[8,64]{1,0:T(8,128)S(1)}, f32[8,64,1536]{2,1,0:T(8,128)S(1)}) fusion(bf16[64,8,128]{2,1,0:T(8,128)(2,1)S(1)} %squeeze.51, bf16[1536,256]{1,0:T(8,128)(2,1)} %param.8, pred[64,1536]{1,0:T(8,128)(4,1)S(1)} %compare_and_fusion), kind=kOutput, calls=%fused_computation.65 | convolution fusion | flops 203685376 | bytes 3770368 | tf_op jit(solution)/shard_map/while/body/eval_jaxpr/thd,kd->htk/dot_general | solution.py:28
  61.1 1.3 fusion.13
  62.5 0.7 fusion.7
  63.2 36.2 %all-gather.5 = f32[16,64,8]{1,2,0:T(8,128)S(1)} all-gather(f32[1,64,8]{1,2,0:T(8,128)S(1)} %bitcast.103), channel_id=3, replica_groups=mesh['groups'=1,'kcol'=16,'qrow'=2] {'kcol'}, dimensions={0}, use_global_device_ids=true | all-gather | bytes 34816 | tf_op jit(solution)/shard_map/all_gather | solution.py:15
  99.4 38.4 %all-gather.4 = f32[16,64,8]{1,2,0:T(8,128)S(1)} all-gather(f32[1,64,8]{1,2,0:T(8,128)S(1)} %bitcast.102), channel_id=2, replica_groups=mesh['groups'=1,'kcol'=16,'qrow'=2] {'kcol'}, dimensions={0}, use_global_device_ids=true | all-gather | bytes 34816 | tf_op jit(solution)/shard_map/all_gather | solution.py:15
  137.9 1.0 slice.53
  139.0 22.3 %while.26 = (s32[]{:T(128)}, f32[64,8]{0,1:T(8,128)S(1)}, f32[64,8]{0,1:T(8,128)S(1)}, f32[64,8,128]{2,1,0:T(8,128)S(1)}, f32[16,64,8]{1,2,0:T(8,128)S(1)}, /*in...) while((s32[]{:T(128)}, f32[64,8]{0,1:T(8,128)S(1)}, ...), condition=%wide.region_4.5_spmd, body=%wide.region_3.4_spmd.sunk | while | flops 199685 | bytes 1339535 | solution.py:20
  139.2 1.0 constant_dynamic-slice_fusion.3
  140.2 0.3 fusion.42
  140.7 1.0 constant_dynamic-slice_fusion.3
  141.7 0.3 fusion.42
  142.2 1.0 constant_dynamic-slice_fusion.3
  143.7 1.0 constant_dynamic-slice_fusion.3
  145.2 1.0 constant_dynamic-slice_fusion.3
  146.6 1.0 constant_dynamic-slice_fusion.3
  147.6 0.3 fusion.42
  148.1 1.0 constant_dynamic-slice_fusion.3
  149.1 0.3 fusion.42
  149.6 1.0 constant_dynamic-slice_fusion.3
  151.1 1.0 constant_dynamic-slice_fusion.3
  152.6 1.0 constant_dynamic-slice_fusion.3
  154.1 1.0 constant_dynamic-slice_fusion.3
  155.6 1.0 constant_dynamic-slice_fusion.3
  157.0 1.0 constant_dynamic-slice_fusion.3
  158.5 1.0 constant_dynamic-slice_fusion.3
  160.0 1.0 constant_dynamic-slice_fusion.3
  161.5 0.6 copy.43
  (73 shorter events, 6.7 us)
Async XLA Ops:
  6.5 131.3 %all-gather.8.cloned.1.call-start = ((), (), s32[]{:S(2)}) async-start(), calls=%async_computation | async-start | bytes 4456448 | tf_op jit(solution)/shard_map/all_gather | solution.py:15
  51.5 9.6 %copy-start = (bf16[1536,256]{1,0:T(8,128)(2,1)S(1)}, bf16[1536,256]{1,0:T(8,128)(2,1)}, u32[]{:S(2)}) copy-start(bf16[1536,256]{1,0:T(8,128)(2,1)} %param.8) | copy-start | bytes 2359300
Sparse Core Ops, SparseCore 0:
  62.6 72.9 all-gather.7
where the time goes:
time: 170 us; the launch traced here: 169 us
  blocking collectives  118 us (69%)
  local copies, waits for them, and re-layouts  19.7 us (12%)
  other arithmetic  14.2 us (8%)
  between operations  13.5 us (8%)
  matrix products  3.06 us (2%)
    all_gather x2, blocking collectives, combined_all(): gathered = jax.tree.map(lambda a: lax.all_gather(a, axis), part)  74.7 us
    all_gather x1, blocking collectives, per_device(): gathered = lax.all_gather(queries, 'kcol', axis=0, tiled=True)  43.3 us
    dynamic_slice x18, local copies, waits for them, and re-layouts, take(): lax.dynamic_index_in_dim(a, source, 0, False)  15.5 us
    gather x1, other arithmetic, one_block(): usable = jnp.repeat(listed_here, BLK, total_repeat_length=stored * BLK)  4.49 us
    add x15, other arithmetic, combine_partials(): numer_left * scale_left[..., None] + numer_right * scale_right[..., None]  4.46 us
  transfers between devices with their start and end apart: 1, of which 0 were waited for; matrix products, arithmetic and copies ran while one was open for 0% of the time, Pallas kernels for 0%

commit v1 on v0

v1 whole, which is shorter than its diff:
```python
import functools
import math

import jax
import jax.numpy as jnp
from jax import lax
from jax.experimental import pallas as pl
from jax.experimental.pallas import tpu as pltpu
from jax.sharding import PartitionSpec as P

BLK = 128
LANES = 128
MASKED = -(2.0**100)
VMEM_LIMIT = 127 * 512 * 1024


def kernel(
    columns,
    cores,
    q_ref,
    kv_hbm,
    lists_ref,
    out_ref,
    kv,
    q_all,
    bias,
    numer,
    stats,
    numer_in,
    stats_in,
    kv_sem,
    q_send,
    q_recv,
    n_send,
    n_recv,
    s_send,
    s_recv,
):
    me = lax.axis_index("kcol")
    core = lax.axis_index("qrow")
    tok_dev, features = q_ref.shape
    head_dim = kv.shape[1] // 2
    heads = features // head_dim
    stored = kv.shape[0] // BLK
    all_blocks = stored * columns
    query_blocks = lists_ref.shape[0]
    rows = tok_dev * heads
    unit_cols = LANES // rows
    units = columns // unit_cols
    tile_cols = BLK // cores // tok_dev
    scale = math.log2(math.e) / math.sqrt(head_dim)

    kv_copy = pltpu.make_async_copy(kv_hbm, kv, kv_sem)
    kv_copy.start()

    barrier = pltpu.get_barrier_semaphore()
    for step in range(1, columns):
        pl.semaphore_signal(
            barrier, inc=1, device_id={"kcol": lax.rem(me + step, columns)}
        )

    def rows_of(column):
        return pl.ds(pl.multiple_of(column * rows, rows), rows)

    own = q_ref[...].astype(jnp.float32)
    own = jnp.concatenate(
        [own[:, h * head_dim : (h + 1) * head_dim] for h in range(heads)], axis=0
    )
    q_all[rows_of(me), :] = own.astype(jnp.bfloat16)

    for tile in range(query_blocks):
        listed = lists_ref[tile : tile + 1, :]
        for block in range(stored):
            hit = jnp.where(listed == me * stored + block, 0.0, MASKED)
            hit = jnp.max(hit, axis=1, keepdims=True)
            bias[tile, :, block * BLK : (block + 1) * BLK] = jnp.broadcast_to(hit, (8, BLK))

    pl.semaphore_wait(barrier, columns - 1)

    my_unit = me // unit_cols
    my_place = lax.rem(me, unit_cols)

    def unit_at(g):
        return lax.rem(my_unit + g, units)

    def column_at(g, j):
        return unit_at(g) * unit_cols + lax.rem(my_place + j, unit_cols)

    def q_copy(peer):
        return pltpu.make_async_remote_copy(
            src_ref=q_all.at[rows_of(me)],
            dst_ref=q_all.at[rows_of(me)],
            send_sem=q_send.at[peer],
            recv_sem=q_recv.at[me],
            device_id={"kcol": peer},
        )

    def q_landed(source):
        return pltpu.make_async_remote_copy(
            src_ref=q_all.at[rows_of(source)],
            dst_ref=q_all.at[rows_of(source)],
            send_sem=q_send.at[source],
            recv_sem=q_recv.at[source],
            device_id={"kcol": source},
        )

    def n_copy(peer, source):
        return pltpu.make_async_remote_copy(
            src_ref=numer.at[rows_of(peer)],
            dst_ref=numer_in.at[rows_of(source)],
            send_sem=n_send.at[peer],
            recv_sem=n_recv.at[source],
            device_id={"kcol": peer},
        )

    def s_copy(peer, source):
        return pltpu.make_async_remote_copy(
            src_ref=stats.at[peer // unit_cols],
            dst_ref=stats_in.at[source],
            send_sem=s_send.at[peer],
            recv_sem=s_recv.at[source],
            device_id={"kcol": peer},
        )

    peers = [(g, j) for g in range(units) for j in range(unit_cols) if g or j]
    for g, j in peers:
        q_copy(column_at(units - g if g else 0, j)).start()

    row_id = lax.broadcasted_iota(jnp.int32, (LANES, LANES), 0)
    lane_id = lax.broadcasted_iota(jnp.int32, (LANES, LANES), 1)
    diagonal = row_id == lane_id
    row_token = core * tok_dev + lax.rem(row_id, tok_dev)
    row_column = row_id // rows

    kv_copy.wait()

    for g in range(units):
        unit = unit_at(g)
        for j in range(unit_cols):
            if g or j:
                q_landed(column_at(g, j)).wait_recv()
        tile = unit * unit_cols // tile_cols
        unit_rows = pl.ds(pl.multiple_of(unit * LANES, LANES), LANES)
        scores = lax.dot_general(
            q_all[unit_rows, :],
            kv[:, :head_dim],
            (((1,), (1,)), ((), ())),
            preferred_element_type=jnp.float32,
        )
        query_pos = (
            (all_blocks - query_blocks) * BLK
            + (unit * unit_cols + row_column) * (cores * tok_dev)
            + row_token
        )
        parts = []
        for block in range(stored):
            part = scores[:, block * BLK : (block + 1) * BLK]
            part = part + bias[tile, 0:1, block * BLK : (block + 1) * BLK]
            if block >= stored - query_blocks:
                key_pos = (me * stored + block) * BLK + lane_id
                part = jnp.where(key_pos <= query_pos, part, MASKED)
            parts.append(part)
        row_max = functools.reduce(jnp.maximum, parts)
        row_max = jnp.max(row_max, axis=1, keepdims=True)
        weights = [jnp.exp2((part - row_max) * scale) for part in parts]
        row_total = jnp.sum(functools.reduce(jnp.add, weights), axis=1, keepdims=True)
        summed = lax.dot_general(
            jnp.concatenate([w.astype(jnp.bfloat16) for w in weights], axis=1),
            kv[:, head_dim:],
            (((1,), (0,)), ((), ())),
            preferred_element_type=jnp.float32,
        )
        numer[unit_rows, :] = summed.astype(jnp.bfloat16)
        stats[unit, 0:1, :] = jnp.sum(jnp.where(diagonal, row_max, 0.0), axis=0, keepdims=True)
        stats[unit, 1:2, :] = jnp.sum(jnp.where(diagonal, row_total, 0.0), axis=0, keepdims=True)
        for j in range(unit_cols):
            if g or j:
                n_copy(column_at(g, j), me).start()
                s_copy(column_at(g, j), me).start()

    numer_in[rows_of(me), :] = numer[rows_of(me), :]
    stats_in[me] = stats[my_unit]

    for g, j in peers:
        source = column_at(units - g if g else 0, j)
        s_copy(source, source).wait_recv()
    every_max = stats_in[:, 0, :]
    every_total = stats_in[:, 1, :]
    top = jnp.max(every_max, axis=0, keepdims=True)
    factor = jnp.exp2((every_max - top) * scale)
    factor = factor / jnp.sum(factor * every_total, axis=0, keepdims=True)
    pad = -columns % LANES
    if pad:
        factor = jnp.concatenate([factor, jnp.zeros((pad, LANES), jnp.float32)], axis=0)
    factor = jnp.transpose(factor)
    turned = jnp.zeros((rows, LANES), jnp.float32)
    for place in range(unit_cols):
        turned = jnp.where(my_place == place, factor[place * rows : (place + 1) * rows, :], turned)

    for g, j in peers:
        source = column_at(units - g if g else 0, j)
        n_copy(source, source).wait_recv()
    total = jnp.zeros((rows, head_dim), jnp.float32)
    for source in range(columns):
        arrived = numer_in[source * rows : (source + 1) * rows, :].astype(jnp.float32)
        total = total + arrived * turned[:, source : source + 1]
    out_ref[...] = jnp.concatenate(
        [total[h * tok_dev : (h + 1) * tok_dev, :] for h in range(heads)], axis=1
    ).astype(out_ref.dtype)

    for g, j in peers:
        peer = column_at(g, j)
        q_copy(peer).wait_send()
        n_copy(peer, me).wait_send()
        s_copy(peer, me).wait_send()


def per_device(columns, cores, queries, key_value, block_lists):
    tok_dev, features = queries.shape
    head_dim = key_value.shape[1] // 2
    all_rows = columns * tok_dev * (features // head_dim)
    query_blocks = block_lists.shape[0]
    units = all_rows // LANES
    dma = pltpu.SemaphoreType.DMA
    vmem = pl.BlockSpec(memory_space=pltpu.VMEM)
    return pl.pallas_call(
        functools.partial(kernel, columns, cores),
        out_shape=jax.ShapeDtypeStruct((tok_dev, features), jnp.bfloat16),
        in_specs=[vmem, pl.BlockSpec(memory_space=pl.ANY), vmem],
        out_specs=vmem,
        scratch_shapes=[
            pltpu.VMEM(key_value.shape, jnp.bfloat16),
            pltpu.VMEM((all_rows, head_dim), jnp.bfloat16),
            pltpu.VMEM((query_blocks, 8, key_value.shape[0]), jnp.float32),
            pltpu.VMEM((all_rows, head_dim), jnp.bfloat16),
            pltpu.VMEM((units, 2, LANES), jnp.float32),
            pltpu.VMEM((all_rows, head_dim), jnp.bfloat16),
            pltpu.VMEM((columns, 2, LANES), jnp.float32),
            dma,
            dma((columns,)),
            dma((columns,)),
            dma((columns,)),
            dma((columns,)),
            dma((columns,)),
            dma((columns,)),
        ],
        compiler_params=pltpu.CompilerParams(
            collective_id=0, has_side_effects=True, vmem_limit_bytes=VMEM_LIMIT
        ),
    )(queries, key_value, block_lists)


def solution(mesh):
    placed = (P(("groups", "kcol", "qrow"), None), P(("groups", "kcol"), None), P("groups", None))
    return jax.shard_map(
        functools.partial(per_device, mesh.shape["kcol"], mesh.shape["qrow"]),
        mesh=mesh,
        in_specs=placed,
        out_specs=P(("groups", "kcol", "qrow"), None),
        check_vma=False,
    )
```

time: 170 us -> 21.1 us (0.12)
  blocking collectives: 118 us -> 0 us
  Pallas kernels: 0 us -> 19.5 us
  local copies, waits for them, and re-layouts: 19.7 us -> 1.3 us
  other arithmetic: 14.2 us -> 0 us
  between operations: 13.5 us -> 0.01 us
  matrix products: 3.06 us -> 0 us
    all_gather x3 -> x0, blocking collectives: 118 us -> none  [the longest x2 74.7 us: combined_all(): gathered = jax.tree.map(lambda a: lax.all_gather(a, axis), part)]
    pallas_call x0 -> x1, Pallas kernels: none -> 19.5 us  [per_device(): pl.pallas_call(functools.partial(kernel, columns, cores), out_shape=jax.S...]
    dynamic_slice x20 -> x0, local copies, waits for them, and re-layouts: 15.7 us -> none  [the longest x18 15.5 us: take(): lax.dynamic_index_in_dim(a, source, 0, False)]
    add x33 -> x0, other arithmetic: 4.72 us -> none  [the longest x15 4.46 us: combine_partials(): numer_left * scale_left[..., None] + numer_right * scale_right[..., None]]
    gather x1 -> x0, other arithmetic: 4.49 us -> none  [one_block(): usable = jnp.repeat(listed_here, BLK, total_repeat_length=stored * BLK)]
    select_n x1 -> x0, other arithmetic: 3.21 us -> none  [one_block(): usable = jnp.repeat(listed_here, BLK, total_repeat_length=stored * BLK)]
    dot_general x2 -> x0, matrix products: 3.06 us -> none  [the longest x1 1.72 us: partial_softmax(): jnp.einsum('thd,kd->htk', query_tile, key_rows, preferred_element_type=jn...]
    exp x30 -> x0, local copies, waits for them, and re-layouts: 2.53 us -> none  [the longest x15 1.27 us: combine_partials(): scale_right = jnp.exp(max_right - row_max)]
  transfers between devices with their start and end apart: 1 -> 0, of which waited for: 0 -> 0; matrix products, arithmetic and copies ran while one was open for 0% -> 0% of each run, Pallas kernels for 0% -> 0%
where the time goes in v1:
time: 21.1 us; the launch traced here: 20.8 us
  Pallas kernels  19.5 us (92%)
  local copies, waits for them, and re-layouts  1.3 us (6%)
    pallas_call x1, Pallas kernels, per_device(): pl.pallas_call(functools.partial(kernel, columns, cores), out_shape=jax.S...  19.5 us
    unnamed x1, local copies, waits for them, and re-layouts  1.3 us

profile of v1, /device:TPU:0, one launch (start us, length us, event | category | flops | bytes accessed | tf_op | source)
XLA Modules:
  0.0 20.8 jit_solution(9068591662227086335)
XLA Ops:
  0.0 19.5 %shard_map.37 = bf16[4,1024]{1,0:T(4,128)(2,1)} custom-call(bf16[4,1024]{1,0:T(4,128)(2,1)} %q_ref.1, bf16[1536,256]{1,0:T(8,128)(2,1)} %kv_hbm.1, s32[1,64]{1,0:T(1,128)} %lists_ref.1), custom_call_target="tpu_custom_call" | custom-call | tf_op jit(solution)/shard_map/pallas_call | solution.py:226
  19.5 1.3 %copy.5 = bf16[4,1024]{1,0:T(4,128)(2,1)} copy(bf16[4,1024]{1,0:T(4,128)(2,1)} %shard_map.37) | data formatting | bytes 16384

commit v2 on v1

--- a/solution.py
+++ b/solution.py
@@ -17,10 +17,12 @@
 def kernel(
     columns,
     cores,
+    q_hbm,
+    kv_hbm,
+    lists_hbm,
+    out_ref,
     q_ref,
-    kv_hbm,
     lists_ref,
-    out_ref,
     kv,
     q_all,
     bias,
@@ -28,7 +30,8 @@
     stats,
     numer_in,
     stats_in,
-    kv_sem,
+    shares,
+    own_sem,
     q_send,
     q_recv,
     n_send,
@@ -50,9 +53,8 @@
     tile_cols = BLK // cores // tok_dev
     scale = math.log2(math.e) / math.sqrt(head_dim)
 
-    kv_copy = pltpu.make_async_copy(kv_hbm, kv, kv_sem)
-    kv_copy.start()
-
+    q_load = pltpu.make_async_copy(q_hbm, q_ref, own_sem.at[0])
+    q_load.start()
     barrier = pltpu.get_barrier_semaphore()
     for step in range(1, columns):
         pl.semaphore_signal(
@@ -62,69 +64,76 @@
     def rows_of(column):
         return pl.ds(pl.multiple_of(column * rows, rows), rows)
 
+    kv_copy = pltpu.make_async_copy(kv_hbm, kv, own_sem.at[1])
+    kv_copy.start()
+    lists_load = pltpu.make_async_copy(lists_hbm, lists_ref, own_sem.at[2])
+    lists_load.start()
+
+    q_load.wait()
     own = q_ref[...].astype(jnp.float32)
     own = jnp.concatenate(
         [own[:, h * head_dim : (h + 1) * head_dim] for h in range(heads)], axis=0
     )
     q_all[rows_of(me), :] = own.astype(jnp.bfloat16)
 
+    pl.semaphore_wait(barrier, columns - 1)
+
+    my_unit = me // unit_cols
+    my_place = lax.rem(me, unit_cols)
+
+    def unit_at(g):
+        return lax.rem(my_unit + g, units)
+
+    def column_at(g, j):
+        return unit_at(g) * unit_cols + lax.rem(my_place + j, unit_cols)
+
+    def q_copy(peer):
+        return pltpu.make_async_remote_copy(
+            src_ref=q_all.at[rows_of(me)],
+            dst_ref=q_all.at[rows_of(me)],
+            send_sem=q_send.at[peer],
+            recv_sem=q_recv.at[me],
+            device_id={"kcol": peer},
+        )
+
+    def q_landed(source):
+        return pltpu.make_async_remote_copy(
+            src_ref=q_all.at[rows_of(source)],
+            dst_ref=q_all.at[rows_of(source)],
+            send_sem=q_send.at[source],
+            recv_sem=q_recv.at[source],
+            device_id={"kcol": source},
+        )
+
+    def n_copy(peer, source):
+        return pltpu.make_async_remote_copy(
+            src_ref=numer.at[rows_of(peer)],
+            dst_ref=numer_in.at[rows_of(source)],
+            send_sem=n_send.at[peer],
+            recv_sem=n_recv.at[source],
+            device_id={"kcol": peer},
+        )
+
+    def s_copy(peer, source):
+        return pltpu.make_async_remote_copy(
+            src_ref=stats.at[peer // unit_cols],
+            dst_ref=stats_in.at[source],
+            send_sem=s_send.at[peer],
+            recv_sem=s_recv.at[source],
+            device_id={"kcol": peer},
+        )
+
+    peers = [(g, j) for g in range(units) for j in range(unit_cols) if g or j]
+    for g, j in peers:
+        q_copy(column_at(units - g if g else 0, j)).start()
+
+    lists_load.wait()
     for tile in range(query_blocks):
         listed = lists_ref[tile : tile + 1, :]
         for block in range(stored):
             hit = jnp.where(listed == me * stored + block, 0.0, MASKED)
             hit = jnp.max(hit, axis=1, keepdims=True)
             bias[tile, :, block * BLK : (block + 1) * BLK] = jnp.broadcast_to(hit, (8, BLK))
-
-    pl.semaphore_wait(barrier, columns - 1)
-
-    my_unit = me // unit_cols
-    my_place = lax.rem(me, unit_cols)
-
-    def unit_at(g):
-        return lax.rem(my_unit + g, units)
-
-    def column_at(g, j):
-        return unit_at(g) * unit_cols + lax.rem(my_place + j, unit_cols)
-
-    def q_copy(peer):
-        return pltpu.make_async_remote_copy(
-            src_ref=q_all.at[rows_of(me)],
-            dst_ref=q_all.at[rows_of(me)],
-            send_sem=q_send.at[peer],
-            recv_sem=q_recv.at[me],
-            device_id={"kcol": peer},
-        )
-
-    def q_landed(source):
-        return pltpu.make_async_remote_copy(
-            src_ref=q_all.at[rows_of(source)],
-            dst_ref=q_all.at[rows_of(source)],
-            send_sem=q_send.at[source],
-            recv_sem=q_recv.at[source],
-            device_id={"kcol": source},
-        )
-
-    def n_copy(peer, source):
-        return pltpu.make_async_remote_copy(
-            src_ref=numer.at[rows_of(peer)],
-            dst_ref=numer_in.at[rows_of(source)],
-            send_sem=n_send.at[peer],
-            recv_sem=n_recv.at[source],
-            device_id={"kcol": peer},
-        )
-
-    def s_copy(peer, source):
-        return pltpu.make_async_remote_copy(
-            src_ref=stats.at[peer // unit_cols],
-            dst_ref=stats_in.at[source],
-            send_sem=s_send.at[peer],
-            recv_sem=s_recv.at[source],
-            device_id={"kcol": peer},
-        )
-
-    peers = [(g, j) for g in range(units) for j in range(unit_cols) if g or j]
-    for g, j in peers:
-        q_copy(column_at(units - g if g else 0, j)).start()
 
     row_id = lax.broadcasted_iota(jnp.int32, (LANES, LANES), 0)
     lane_id = lax.broadcasted_iota(jnp.int32, (LANES, LANES), 1)
@@ -164,6 +173,11 @@
         row_max = jnp.max(row_max, axis=1, keepdims=True)
         weights = [jnp.exp2((part - row_max) * scale) for part in parts]
         row_total = jnp.sum(functools.reduce(jnp.add, weights), axis=1, keepdims=True)
+        stats[unit, 0:1, :] = jnp.sum(jnp.where(diagonal, row_max, 0.0), axis=0, keepdims=True)
+        stats[unit, 1:2, :] = jnp.sum(jnp.where(diagonal, row_total, 0.0), axis=0, keepdims=True)
+        for j in range(unit_cols):
+            if g or j:
+                s_copy(column_at(g, j), me).start()
         summed = lax.dot_general(
             jnp.concatenate([w.astype(jnp.bfloat16) for w in weights], axis=1),
             kv[:, head_dim:],
@@ -171,12 +185,9 @@
             preferred_element_type=jnp.float32,
         )
         numer[unit_rows, :] = summed.astype(jnp.bfloat16)
-        stats[unit, 0:1, :] = jnp.sum(jnp.where(diagonal, row_max, 0.0), axis=0, keepdims=True)
-        stats[unit, 1:2, :] = jnp.sum(jnp.where(diagonal, row_total, 0.0), axis=0, keepdims=True)
         for j in range(unit_cols):
             if g or j:
                 n_copy(column_at(g, j), me).start()
-                s_copy(column_at(g, j), me).start()
 
     numer_in[rows_of(me), :] = numer[rows_of(me), :]
     stats_in[me] = stats[my_unit]
@@ -197,13 +208,20 @@
     for place in range(unit_cols):
         turned = jnp.where(my_place == place, factor[place * rows : (place + 1) * rows, :], turned)
 
+    for source in range(columns):
+        shares[source * rows : (source + 1) * rows, :] = jnp.broadcast_to(
+            turned[:, source : source + 1], (rows, head_dim)
+        )
+
+    def share(source):
+        part = numer_in[rows_of(source), :].astype(jnp.float32)
+        return part * shares[rows_of(source), :]
+
+    total = share(me)
     for g, j in peers:
         source = column_at(units - g if g else 0, j)
         n_copy(source, source).wait_recv()
-    total = jnp.zeros((rows, head_dim), jnp.float32)
-    for source in range(columns):
-        arrived = numer_in[source * rows : (source + 1) * rows, :].astype(jnp.float32)
-        total = total + arrived * turned[:, source : source + 1]
+        total = total + share(source)
     out_ref[...] = jnp.concatenate(
         [total[h * tok_dev : (h + 1) * tok_dev, :] for h in range(heads)], axis=1
     ).astype(out_ref.dtype)
@@ -222,13 +240,15 @@
     query_blocks = block_lists.shape[0]
     units = all_rows // LANES
     dma = pltpu.SemaphoreType.DMA
-    vmem = pl.BlockSpec(memory_space=pltpu.VMEM)
+    hbm = pl.BlockSpec(memory_space=pltpu.HBM)
     return pl.pallas_call(
         functools.partial(kernel, columns, cores),
         out_shape=jax.ShapeDtypeStruct((tok_dev, features), jnp.bfloat16),
-        in_specs=[vmem, pl.BlockSpec(memory_space=pl.ANY), vmem],
-        out_specs=vmem,
+        in_specs=[hbm, hbm, hbm],
+        out_specs=pl.BlockSpec(memory_space=pltpu.VMEM),
         scratch_shapes=[
+            pltpu.VMEM(queries.shape, jnp.bfloat16),
+            pltpu.VMEM(block_lists.shape, jnp.int32),
             pltpu.VMEM(key_value.shape, jnp.bfloat16),
             pltpu.VMEM((all_rows, head_dim), jnp.bfloat16),
             pltpu.VMEM((query_blocks, 8, key_value.shape[0]), jnp.float32),
@@ -236,7 +256,8 @@
             pltpu.VMEM((units, 2, LANES), jnp.float32),
             pltpu.VMEM((all_rows, head_dim), jnp.bfloat16),
             pltpu.VMEM((columns, 2, LANES), jnp.float32),
-            dma,
+            pltpu.VMEM((all_rows, head_dim), jnp.float32),
+            dma((3,)),
             dma((columns,)),
             dma((columns,)),
             dma((columns,)),

time: 21.1 us -> 20.2 us (0.957)
  Pallas kernels: 19.5 us -> 18.6 us
    pallas_call x1, Pallas kernels: 19.5 us -> 18.6 us  [per_device(): pl.pallas_call(functools.partial(kernel, columns, cores), out_shape=jax.S...]
where the time goes in v2:
time: 20.2 us; the launch traced here: 19.9 us
  Pallas kernels  18.6 us (92%)
  local copies, waits for them, and re-layouts  1.3 us (6%)
    pallas_call x1, Pallas kernels, per_device(): pl.pallas_call(functools.partial(kernel, columns, cores), out_shape=jax.S...  18.6 us
    unnamed x1, local copies, waits for them, and re-layouts  1.3 us

profile of v2, /device:TPU:0, one launch (start us, length us, event | category | flops | bytes accessed | tf_op | source)
XLA Modules:
  0.0 19.9 jit_solution(10288337853357640223)
XLA Ops:
  0.0 18.6 %shard_map.37 = bf16[4,1024]{1,0:T(4,128)(2,1)} custom-call(bf16[4,1024]{1,0:T(4,128)(2,1)} %q_hbm.1, bf16[1536,256]{1,0:T(8,128)(2,1)} %kv_hbm.1, s32[1,64]{1,0:T(1,128)} %lists_hbm.1), custom_call_target="tpu_custom_call" | custom-call | tf_op jit(solution)/shard_map/pallas_call | solution.py:244
  18.6 1.3 %copy.5 = bf16[4,1024]{1,0:T(4,128)(2,1)} copy(bf16[4,1024]{1,0:T(4,128)(2,1)} %shard_map.37) | data formatting | bytes 16384

commit v3 on v2

--- a/solution.py
+++ b/solution.py
@@ -200,17 +200,11 @@
     top = jnp.max(every_max, axis=0, keepdims=True)
     factor = jnp.exp2((every_max - top) * scale)
     factor = factor / jnp.sum(factor * every_total, axis=0, keepdims=True)
-    pad = -columns % LANES
-    if pad:
-        factor = jnp.concatenate([factor, jnp.zeros((pad, LANES), jnp.float32)], axis=0)
-    factor = jnp.transpose(factor)
-    turned = jnp.zeros((rows, LANES), jnp.float32)
-    for place in range(unit_cols):
-        turned = jnp.where(my_place == place, factor[place * rows : (place + 1) * rows, :], turned)
-
+    mine = row_id[:rows] + my_place * rows == lane_id[:rows]
     for source in range(columns):
+        picked = jnp.where(mine, factor[source : source + 1, :], 0.0)
         shares[source * rows : (source + 1) * rows, :] = jnp.broadcast_to(
-            turned[:, source : source + 1], (rows, head_dim)
+            jnp.sum(picked, axis=1, keepdims=True), (rows, head_dim)
         )
 
     def share(source):

time: 20.2 us -> 20.2 us (level)
  no operation moved by 1% of the time
where the time goes in v3:
time: 20.2 us; the launch traced here: 19.9 us
  Pallas kernels  18.6 us (92%)
  local copies, waits for them, and re-layouts  1.3 us (6%)
    pallas_call x1, Pallas kernels, per_device(): pl.pallas_call(functools.partial(kernel, columns, cores), out_shape=jax.S...  18.6 us
    unnamed x1, local copies, waits for them, and re-layouts  1.3 us

profile of v3, /device:TPU:0, one launch (start us, length us, event | category | flops | bytes accessed | tf_op | source)
XLA Modules:
  0.0 19.9 jit_solution(14780663420961280755)
XLA Ops:
  0.0 18.6 %shard_map.37 = bf16[4,1024]{1,0:T(4,128)(2,1)} custom-call(bf16[4,1024]{1,0:T(4,128)(2,1)} %q_hbm.1, bf16[1536,256]{1,0:T(8,128)(2,1)} %kv_hbm.1, s32[1,64]{1,0:T(1,128)} %lists_hbm.1), custom_call_target="tpu_custom_call" | custom-call | tf_op jit(solution)/shard_map/pallas_call | solution.py:238
  18.6 1.3 %copy.5 = bf16[4,1024]{1,0:T(4,128)(2,1)} copy(bf16[4,1024]{1,0:T(4,128)(2,1)} %shard_map.37) | data formatting | bytes 16384
